TPU v7x, 512 devices: a whole 4x8x8 slice. The times are simulated.
512 devices in a mesh: tile: 64 (over x, z, core), red: 8 (over y).
Axes of the slice: x: 4, y: 8, z: 8, core: 2. Of those that a mesh axis runs over, the one named last changes fastest.
Arguments:
- amplitudes: bfloat16 [16, 64, 1024, 1024], P('red', None, 'tile'), may hold values from -6 to 6
- intermediate: bfloat16 [1024, 16, 1024], P(None, 'red'), may hold values from -0.09375 to 0.09375
- contract_irrep: int32 [16], P('red'), may hold values from 0 to 3
- column_irrep: int32 [64], replicated, may hold values from 0 to 3
- virtual_irrep: int32 [8], replicated, may hold values from 0 to 3, as said below
Outputs:
- cycle_residual: bfloat16 [1024, 64, 1024], P('red', 'tile')
Inputs may be any that keep to these rules, and one draw needn't show every extreme that they name: `virtual_irrep`: the four irreps label 8 // 2, 2, 1 and 1 of the virtual tiles; which irrep has which count, and which tiles it labels, differ from draw to draw.
All inputs are finite; a program needn't handle non-finite values.
Results may differ from a plain program's by a relative error of at most 0.017.
Values may be sent and summed in bfloat16 or wider, within the bound.
A program may use at most 64 MiB of HBM per device.

v0:
```python
import jax
import jax.numpy as jnp
from jax import lax
from jax.sharding import PartitionSpec as P

TILE = 128


def local(amplitudes, intermediate, contract_irrep, column_irrep, virtual_irrep):
    tile_labels = jnp.repeat(virtual_irrep, TILE)
    width = tile_labels.shape[0]
    shard_c = amplitudes.shape[2]
    c_offset = lax.axis_index("tile") * shard_c
    own_c = lax.dynamic_slice_in_dim(tile_labels, c_offset, shard_c, 0)
    label = jnp.bitwise_xor(
        jnp.bitwise_xor(contract_irrep[:, None, None, None], column_irrep[None, :, None, None]),
        jnp.bitwise_xor(own_c[None, None, :, None], tile_labels[None, None, None, :]),
    )
    masked = jnp.where(label == 0, amplitudes, jnp.zeros_like(amplitudes))
    red_rows = width // lax.axis_size("red")
    cols_here = column_irrep.shape[0] // lax.axis_size("tile")
    regrouped = lax.all_to_all(masked, "tile", split_axis=1, concat_axis=2, tiled=True)
    summed = lax.psum_scatter(
        jnp.einsum(
            "akc,kjcb->ajb", intermediate, regrouped, preferred_element_type=jnp.float32
        ).astype(jnp.bfloat16),
        "red",
        scatter_dimension=0,
        tiled=True,
    ).astype(jnp.float32)
    own_rows = lax.dynamic_slice_in_dim(tile_labels, lax.axis_index("red") * red_rows, red_rows, 0)
    own_cols = lax.dynamic_slice_in_dim(
        column_irrep, lax.axis_index("tile") * cols_here, cols_here, 0
    )
    label_out = jnp.bitwise_xor(
        jnp.bitwise_xor(own_rows[:, None, None], own_cols[None, :, None]),
        tile_labels[None, None, :],
    )
    return jnp.where(label_out == 0, summed, 0.0).astype(jnp.bfloat16)


def solution(mesh):
    in_specs = (P("red", None, "tile", None), P(None, "red", None), P("red"), P(), P())
    out_specs = P("red", "tile", None)
    return jax.shard_map(local, mesh=mesh, in_specs=in_specs, out_specs=out_specs, check_vma=False)
```

profile of v0, /device:TPU:1, one launch (start us, length us, event | category | flops | bytes accessed | tf_op | source)
XLA Modules:
  0.0 178.1 jit_solution(5539829173324996112)
XLA Ops:
  6.5 0.0 copy-start
  6.5 0.0 reduce-scatter.4.cloned.1.call-start
  6.5 0.7 copy-done
  7.2 0.1 broadcast_bitcast_fusion
  7.3 0.1 dynamic_slice.11
  7.3 0.1 broadcast_xor_fusion
  7.4 0.7 broadcast_xor_fusion.1
  8.2 3.0 %fusion = bf16[2,64,16,1024]{3,2,0,1:T(8,128)(2,1)S(1)} fusion(bf16[2,64,16,1024]{3,2,1,0:T(8,128)(2,1)} %param.5, s32[16,1024]{1,0:T(8,128)S(1)} %broadcast_xor_fusion, s32[2,64]{0,1:T(8,128)S(1)} %broadcast_xor_fusion.1), kind=kLoop, calls=%fused_computation.1 | loop fusion | flops 6291456 | bytes 8454656 | tf_op jit(solution)/shard_map/jit(_where)/select_n | solution.py:19
  11.2 110.8 %all_to_all.4 = bf16[2,64,16,1024]{3,2,0,1:T(8,128)(2,1)S(1)} all-to-all(bf16[2,64,16,1024]{3,2,0,1:T(8,128)(2,1)S(1)} %fusion), channel_id=1, replica_groups=mesh['tile'=64,'red'=8] {'tile'}, dimensions={1} | all-to-all | bytes 8388608 | tf_op jit(solution)/shard_map/all_to_all | solution.py:22
  122.0 0.0 copy-start.2
  122.0 0.8 copy.13
  122.8 1.3 copy-done.2
  124.2 5.3 %fusion.3 = bf16[1024,1024]{0,1:T(8,128)(2,1)S(1)} fusion(bf16[2,1024,1024]{2,1,0:T(8,128)(2,1)S(1)} %bitcast.18, bf16[1024,2,1024]{2,1,0:T(2,128)(2,1)S(1)} %copy-done.2), kind=kOutput, calls=%fused_computation.5 | convolution fusion | flops 4296015872 | bytes 10485760 | tf_op jit(solution)/shard_map/akc,kjcb->ajb/dot_general | solution.py:24
  129.5 0.0 copy-start.1
  129.5 2.6 %copy.20 = bf16[1024,1024]{1,0:T(8,128)(2,1)} copy(bf16[1024,1024]{0,1:T(8,128)(2,1)S(1)} %fusion.3) | data formatting | bytes 4194304
  132.0 0.0 reduce-scatter.4.cloned.1.call-update
  132.1 0.0 copy-done.1
  132.1 0.6 dynamic_slice.10
  132.7 0.7 dynamic-slice_xor_fusion
  133.4 35.7 %reduce-scatter.4.cloned.1.call-done = bf16[128,1024]{1,0:T(8,128)(2,1)} async-done(((bf16[1024,1024]{1,0:T(8,128)(2,1)}), bf16[128,1024]{1,0:T(8,128)(2,1)}) %reduce-scatter.4.cloned.1.call-update) | async-done | bytes 262160
  169.1 1.1 copy.21
  170.2 0.2 select_convert_fusion
  170.4 0.9 copy.16
Async XLA Ops:
  6.5 0.7 copy-start
  6.5 162.6 %reduce-scatter.4.cloned.1.call-start = ((), (), s32[]{:S(2)}) async-start(), calls=%async_computation.2 | async-start | bytes 2359296
  122.0 2.2 %copy-start.2 = (bf16[1024,2,1024]{2,1,0:T(2,128)(2,1)S(1)}, bf16[1024,2,1024]{2,1,0:T(2,128)(2,1)}, u32[]{:S(2)}) copy-start(bf16[1024,2,1024]{2,1,0:T(2,128)(2,1)} %param.6) | copy-start | bytes 12582916
  129.5 2.6 %copy-start.1 = (s32[64]{0:T(128)S(1)}, s32[64]{0:T(128)}, u32[]{:S(2)}) copy-start(s32[64]{0:T(128)} %param.8) | copy-start | bytes 772
Sparse Core Ops, SparseCore 0:
  132.2 36.8 reduce-scatter.3
where the time goes:
time: 181 us; the launch traced here: 178 us
  blocking collectives  111 us (61%)
  waiting for transfers between devices  35.7 us (20%)
  between operations  13.5 us (7%)
  local copies, waits for them, and re-layouts  8.11 us (4%)
  matrix products  5.25 us (3%)
  other arithmetic  4.76 us (3%)
    all_to_all x1, blocking collectives, local(): lax.all_to_all(masked, 'tile', split_axis=1, concat_axis=2, tiled=True)  111 us
    unnamed x2, waiting for transfers between devices  35.7 us
    unnamed x8, local copies, waits for them, and re-layouts  5.69 us
    dot_general x1, matrix products, local(): jnp.einsum('akc,kjcb->ajb', intermediate, regrouped, preferred_element_ty...  5.25 us
  transfers between devices with their start and end apart: 1, of which 1 were waited for; matrix products, arithmetic and copies ran while one was open for 1% of the time, Pallas kernels for 0%

commit v1 on v0

v1 whole, which is shorter than its diff:
```python
import functools

import jax
import jax.numpy as jnp
from jax import lax
from jax.experimental import pallas as pl
from jax.experimental.pallas import tpu as pltpu
from jax.sharding import PartitionSpec as P

TILE = 128
SLOTS = 4
CHUNKS = 4
MESH = pl.DeviceIdType.MESH


def peer(me, n, dims):
    xs, zs, cs = dims
    core, z, x = me % cs, (me // cs) % zs, me // (cs * zs)
    m = n % zs
    dz = ((m + 1) // 2) * (2 * (m % 2) - 1) + zs
    rest = n // zs
    dcore, dx = rest % cs, rest // cs
    return ((x + dx) % xs * zs + (z + dz) % zs) * cs + (core + dcore) % cs


def tile_ranks(lv, ntiles):
    labels = [lv[v] for v in range(ntiles)]
    ranks = []
    for v in range(ntiles):
        rank = jnp.int32(0)
        for u in range(v):
            rank = rank + jnp.where(labels[u] == labels[v], 1, 0)
        ranks.append(rank)
    return labels, ranks


def pack_kernel(ck, cj, lv, where, t, out, tab):
    n_k, n_j, rows, width = t.shape
    per = SLOTS // CHUNKS

    @pl.when(pl.program_id(0) == 0)
    def _():
        labels, ranks = tile_ranks(lv, width // TILE)
        for s in range(4):
            for i in range(SLOTS):
                pos = jnp.int32(0)
                for v in range(width // TILE):
                    pos = jnp.where((labels[v] == s) & (ranks[v] == i), v, pos)
                tab[s * SLOTS + i] = pos

    own_label = lv[where[0]]

    def step(j, carry):
        for k in range(n_k):
            s = ck[k] ^ cj[pl.program_id(0) * n_j + j] ^ own_label
            for i in range(SLOTS):
                tile = tab[s * SLOTS + i]
                q = i % per
                out[i // per, j, k, :, q * TILE:(q + 1) * TILE] = t[
                    k, j, :, pl.ds(pl.multiple_of(tile * TILE, TILE), TILE)]
        return carry

    lax.fori_loop(0, n_j, step, 0, unroll=4)


def unpack_kernel(cj, lv, where, packed, out):
    ntiles = out.shape[1] // TILE
    labels, ranks = tile_ranks(lv, ntiles)
    want = lv[where[1]] ^ cj[where[0]]
    for v in range(ntiles):
        block = packed[:, pl.ds(pl.multiple_of(ranks[v] * TILE, TILE), TILE)]
        keep = jnp.broadcast_to(labels[v] == want, block.shape)
        out[:, v * TILE:(v + 1) * TILE] = jnp.where(keep, block, jnp.zeros_like(block))


def kernel(dims, n_tile, n_red, pk, w_hbm, out, wv, recv, part, ybuf,
           w_sem, send_sem, recv_sem, own_sem, ysend_sem, yrecv_sem):
    me, my = lax.axis_index("tile"), lax.axis_index("red")
    n_k, rows = pk.shape[2], pk.shape[3]
    width = wv.shape[0]
    cw = pk.shape[4]
    w_copy = pltpu.make_async_copy(w_hbm, wv, w_sem)
    w_copy.start()

    barrier = pltpu.get_barrier_semaphore()

    def greet(n, carry):
        pl.semaphore_signal(barrier, inc=1, device_id=(peer(me, n, dims), my), device_id_type=MESH)
        return carry

    def greet_red(n, carry):
        pl.semaphore_signal(barrier, inc=1, device_id=(me, (my + n) % n_red), device_id_type=MESH)
        return carry

    lax.fori_loop(1, n_tile, greet, 0)
    lax.fori_loop(1, n_red, greet_red, 0)
    pl.semaphore_wait(barrier, n_tile + n_red - 2)

    own_rows = pl.ds(pl.multiple_of(me * rows, rows), rows)
    own = []
    for i in range(CHUNKS):
        def step(n, carry, i=i):
            j = peer(me, n, dims)
            pltpu.make_async_remote_copy(
                src_ref=pk.at[i, j],
                dst_ref=recv.at[i, :, own_rows, :],
                send_sem=send_sem.at[i],
                recv_sem=recv_sem.at[i],
                device_id=(j, my),
                device_id_type=MESH,
            ).start()
            return carry
        lax.fori_loop(1, n_tile, step, 0)
        copy = pltpu.make_async_copy(pk.at[i, me], recv.at[i, :, own_rows, :], own_sem.at[i])
        copy.start()
        own.append(copy)

    w_copy.wait()
    for i in range(CHUNKS):
        own[i].wait()
        others = recv.at[i, :, pl.ds(0, (n_tile - 1) * rows), :]
        pltpu.make_async_copy(others, others, recv_sem.at[i]).wait()

        def multiply(n, carry, i=i):
            to = (my + n) % n_red
            a_rows = pl.ds(pl.multiple_of(to * TILE, TILE), TILE)
            acc = jnp.dot(wv[a_rows, :width], recv[i, 0], preferred_element_type=jnp.float32)
            for k in range(1, n_k):
                acc += jnp.dot(wv[a_rows, k * width:(k + 1) * width], recv[i, k],
                               preferred_element_type=jnp.float32)
            part[i, to] = acc.astype(part.dtype)

            @pl.when(n < n_red)
            def _():
                pltpu.make_async_remote_copy(
                    src_ref=part.at[i, to],
                    dst_ref=ybuf.at[i, my],
                    send_sem=ysend_sem.at[i],
                    recv_sem=yrecv_sem.at[i],
                    device_id=(me, to),
                    device_id_type=MESH,
                ).start()
            return carry

        lax.fori_loop(1, n_red + 1, multiply, 0)

    for i in range(CHUNKS):
        others = ybuf.at[i, pl.ds(0, n_red - 1)]
        pltpu.make_async_copy(others, others, yrecv_sem.at[i]).wait()
        total = part[i, my].astype(jnp.float32)
        for d in range(1, n_red):
            total += ybuf[i, (my + d) % n_red].astype(jnp.float32)
        out[:, i * cw:(i + 1) * cw] = total.astype(out.dtype)

    for i in range(CHUNKS):
        sent = pk.at[i, pl.ds(0, n_tile - 1)]
        pltpu.make_async_copy(sent, sent, send_sem.at[i]).wait()
        sent = part.at[i, pl.ds(0, n_red - 1)]
        pltpu.make_async_copy(sent, sent, ysend_sem.at[i]).wait()


def local(n_tile, n_red, amplitudes, intermediate, contract_irrep, column_irrep, virtual_irrep):
    n_k, n_j, rows, width = amplitudes.shape
    me, my = lax.axis_index("tile"), lax.axis_index("red")
    dims = (4, 8, 2) if n_tile == 64 else (1, n_tile // 2, 2)
    cw = SLOTS // CHUNKS * TILE
    bf = jnp.bfloat16
    smem = pl.BlockSpec(memory_space=pltpu.SMEM)
    hbm = pl.BlockSpec(memory_space=pl.ANY)
    vmem = pl.BlockSpec(memory_space=pltpu.VMEM)

    group = 8
    packed = pl.pallas_call(
        pack_kernel,
        out_shape=jax.ShapeDtypeStruct((CHUNKS, n_j, n_k, rows, cw), bf),
        grid=(n_j // group,),
        in_specs=[smem, smem, smem, smem, pl.BlockSpec((n_k, group, rows, width), lambda g: (0, g, 0, 0))],
        out_specs=pl.BlockSpec((CHUNKS, group, n_k, rows, cw), lambda g: (0, g, 0, 0, 0)),
        scratch_shapes=[pltpu.SMEM((4 * SLOTS,), jnp.int32)],
    )(contract_irrep, column_irrep, virtual_irrep, jnp.reshape(me * rows // TILE, (1,)), amplitudes)

    tile_labels = jnp.repeat(virtual_irrep, TILE)
    label = tile_labels[:, None, None] ^ contract_irrep[None, :, None] ^ tile_labels[None, None, :]
    weight = jnp.where(label == 0, intermediate, jnp.zeros_like(intermediate)).reshape(width, n_k * width)

    summed = pl.pallas_call(
        functools.partial(kernel, dims, n_tile, n_red),
        out_shape=jax.ShapeDtypeStruct((TILE, SLOTS * TILE), bf),
        in_specs=[hbm, hbm],
        out_specs=vmem,
        scratch_shapes=[
            pltpu.VMEM((width, n_k * width), bf),
            pltpu.VMEM((CHUNKS, n_k, width, cw), bf),
            pltpu.VMEM((CHUNKS, n_red, TILE, cw), bf),
            pltpu.VMEM((CHUNKS, n_red, TILE, cw), bf),
            pltpu.SemaphoreType.DMA,
            pltpu.SemaphoreType.DMA((CHUNKS,)),
            pltpu.SemaphoreType.DMA((CHUNKS,)),
            pltpu.SemaphoreType.DMA((CHUNKS,)),
            pltpu.SemaphoreType.DMA((CHUNKS,)),
            pltpu.SemaphoreType.DMA((CHUNKS,)),
        ],
        compiler_params=pltpu.CompilerParams(
            collective_id=0, has_side_effects=True, vmem_limit_bytes=48 * 2**20
        ),
        cost_estimate=pl.CostEstimate(flops=2 * width**2 * n_k * SLOTS * TILE, bytes_accessed=9 * 2**20,
                                      transcendentals=0),
    )(packed, weight)

    out = pl.pallas_call(
        unpack_kernel,
        out_shape=jax.ShapeDtypeStruct((TILE, width), bf),
        in_specs=[smem, smem, smem, vmem],
        out_specs=vmem,
    )(column_irrep, virtual_irrep, jnp.stack([me, my]), summed)
    return out[:, None, :]


def solution(mesh):
    in_specs = (P("red", None, "tile", None), P(None, "red", None), P("red"), P(), P())
    out_specs = P("red", "tile", None)
    body = functools.partial(local, mesh.shape["tile"], mesh.shape["red"])
    return jax.shard_map(body, mesh=mesh, in_specs=in_specs, out_specs=out_specs, check_vma=False)
```

time: 181 us -> 98.9 us (0.55); the launches traced: 178 us -> 98.5 us
  blocking collectives: 111 us -> 0 us
  Pallas kernels: 0 us -> 84.2 us
  waiting for transfers between devices: 35.7 us -> 0 us
  between operations: 13.5 us -> 0.04 us
  matrix products: 5.25 us -> 0 us
  other arithmetic: 4.76 us -> 9.51 us
  local copies, waits for them, and re-layouts: 8.11 us -> 4.74 us
    all_to_all x1 -> x0, blocking collectives: 111 us -> none  [local(): lax.all_to_all(masked, 'tile', split_axis=1, concat_axis=2, tiled=True)]
    pallas_call x0 -> x3, Pallas kernels: none -> 84.2 us  [the longest x1 75.6 us: local(): pl.pallas_call(functools.partial(kernel, dims, n_tile, n_red), out_shape=...]
    unnamed x2 -> x0, waiting for transfers between devices: 35.7 us -> none
    dot_general x1 -> x0, matrix products: 5.25 us -> none  [local(): jnp.einsum('akc,kjcb->ajb', intermediate, regrouped, preferred_element_ty...]
    select_n x1, other arithmetic: 3.02 us -> 8.02 us  [local(): jnp.where(label == 0, intermediate, jnp.zeros_like(intermediate))]
    unnamed x8 -> x5, local copies, waits for them, and re-layouts: 5.69 us -> 4.02 us
  transfers between devices with their start and end apart: 1 -> 0, of which waited for: 1 -> 0; matrix products, arithmetic and copies ran while one was open for 1% -> 0% of each run, Pallas kernels for 0% -> 0%
where the time goes in v1:
time: 98.9 us; the launch traced here: 98.5 us
  Pallas kernels  84.2 us (85%)
  other arithmetic  9.51 us (10%)
  local copies, waits for them, and re-layouts  4.74 us (5%)
    pallas_call x1, Pallas kernels, local(): pl.pallas_call(functools.partial(kernel, dims, n_tile, n_red), out_shape=...  75.6 us
    select_n x1, other arithmetic, local(): jnp.where(label == 0, intermediate, jnp.zeros_like(intermediate))  8.02 us
    pallas_call x1, Pallas kernels, local(): pl.pallas_call(pack_kernel, out_shape=jax.ShapeDtypeStruct((CHUNKS, n_j,...  6.83 us
    unnamed x5, local copies, waits for them, and re-layouts  4.02 us

profile of v1, /device:TPU:1, one launch (start us, length us, event | category | flops | bytes accessed | tf_op | source)
XLA Modules:
  0.0 98.5 jit_solution(5931741886027241078)
XLA Ops:
  0.0 0.6 pad_add_fusion.where
  0.6 0.7 broadcast_bitcast_fusion
  1.4 0.8 broadcast_xor_fusion
  2.2 6.8 %shard_map.55.pk = bf16[4,64,2,16,128]{4,3,2,1,0:T(8,128)(2,1)} custom-call(s32[2]{0:T(128)} %ck.1, s32[64]{0:T(128)} %cj.3, s32[8]{0:T(128)} %lv.3, s32[1]{0:T(128)} %bitcast.2.where, bf16[2,64,16,1024]{3,2,1,0:T(8,128)(2,1)} %t.1), custom_call_target="tpu_custom_call" | custom-call | tf_op jit(solution)/shard_map/pallas_call | solution.py:173
  9.1 8.0 %compare_select_fusion = bf16[1024,2,1024]{2,1,0:T(2,128)(2,1)S(1)} fusion(bf16[1024,2,1024]{2,1,0:T(2,128)(2,1)} %param.6, s32[1024]{0:T(1024)S(1)} %broadcast_bitcast_fusion, s32[1024,2]{1,0:T(8,128)S(1)} %broadcast_xor_fusion), kind=kLoop, calls=%fused_computation | loop fusion | flops 6291456 | bytes 8400896 | tf_op jit(solution)/shard_map/jit(_where)/select_n | solution.py:184
  17.1 0.0 copy-start
  17.1 3.4 %copy.6 = bf16[128,8,2,1024]{3,1,2,0:T(8,128)(2,1)} copy(bf16[128,8,2,1024]{3,2,1,0:T(2,128)(2,1)S(1)} %bitcast.8) | data formatting | bytes 8388608
  20.5 0.0 copy-done
  20.5 75.6 %shard_map.56.packed = bf16[128,512]{1,0:T(8,128)(2,1)S(1)} custom-call(bf16[4,64,2,16,128]{4,3,2,1,0:T(8,128)(2,1)S(1)} %copy-done, bf16[1024,2048]{1,0:T(8,128)(2,1)} %bitcast.9), custom_call_target="tpu_custom_call" | custom-call | flops 2147483648 | bytes 9437184 | tf_op jit(solution)/shard_map/pallas_call | solution.py:186
  96.1 0.0 copy-start.1
  96.2 0.6 copy-done.1
  96.8 1.7 %shard_map.57 = bf16[128,1024]{1,0:T(8,128)(2,1)} custom-call(s32[64]{0:T(128)} %cj.3, s32[8]{0:T(128)} %lv.3, s32[2]{0:T(128)} %pad_add_fusion.where, bf16[128,512]{1,0:T(8,128)(2,1)} %copy-done.1), custom_call_target="tpu_custom_call" | custom-call | tf_op jit(solution)/shard_map/pallas_call | solution.py:210
Async XLA Ops:
  17.1 3.4 %copy-start = (bf16[4,64,2,16,128]{4,3,2,1,0:T(8,128)(2,1)S(1)}, bf16[4,64,2,16,128]{4,3,2,1,0:T(8,128)(2,1)}, u32[]{:S(2)}) copy-start(bf16[4,64,2,16,128]{4,3,2,1,0:T(8,128)(2,1)} %shard_map.55.pk) | copy-start | bytes 6291460
  96.1 0.6 copy-start.1

commit v2 on v1

v2 whole, which is shorter than its diff:
```python
import functools

import jax
import jax.numpy as jnp
from jax import lax
from jax.experimental import pallas as pl
from jax.experimental.pallas import tpu as pltpu
from jax.sharding import PartitionSpec as P

TILE = 128
SLOTS = 4
CHUNKS = 4
HALVED = 2
ORDER = (("multiply", 0), ("multiply", 1), ("cross", 0), ("multiply", 2), ("cross", 1), ("multiply", 3),
         ("finish", 0), ("finish", 1), ("finish", 2), ("finish", 3))
MESH = pl.DeviceIdType.MESH


def peer(me, n, dims):
    xs, zs, cs = dims
    core, z, x = me % cs, (me // cs) % zs, me // (cs * zs)
    m = n % zs
    dz = ((m + 1) // 2) * (2 * (m % 2) - 1) + zs
    rest = n // zs
    dcore, dx = rest % cs, rest // cs
    return ((x + dx) % xs * zs + (z + dz) % zs) * cs + (core + dcore) % cs


def tile_ranks(lv, ntiles):
    labels = [lv[v] for v in range(ntiles)]
    ranks = []
    for v in range(ntiles):
        rank = jnp.int32(0)
        for u in range(v):
            rank = rank + jnp.where(labels[u] == labels[v], 1, 0)
        ranks.append(rank)
    return labels, ranks


def pack_kernel(ck, cj, lv, where, t, out, keep, tab):
    n_k, n_j, rows, width = t.shape
    per = SLOTS // CHUNKS
    ntiles = width // TILE

    @pl.when(pl.program_id(0) == 0)
    def _():
        labels, ranks = tile_ranks(lv, width // TILE)
        for s in range(4):
            for i in range(SLOTS):
                pos = jnp.int32(0)
                for v in range(width // TILE):
                    pos = jnp.where((labels[v] == s) & (ranks[v] == i), v, pos)
                tab[s * SLOTS + i] = pos
        for a in range(ntiles):
            for k in range(n_k):
                for c in range(ntiles):
                    fits = jnp.where(labels[a] ^ labels[c] == ck[k], 1.0, 0.0)
                    keep[a, k:k + 1, c * TILE:(c + 1) * TILE] = jnp.full((1, TILE), fits, jnp.float32)

    own_label = lv[where[0]]

    def step(j, carry):
        for k in range(n_k):
            s = ck[k] ^ cj[pl.program_id(0) * n_j + j] ^ own_label
            for i in range(SLOTS):
                tile = tab[s * SLOTS + i]
                q = i % per
                out[i // per, j, k, :, q * TILE:(q + 1) * TILE] = t[
                    k, j, :, pl.ds(pl.multiple_of(tile * TILE, TILE), TILE)]
        return carry

    lax.fori_loop(0, n_j, step, 0, unroll=4)


def unpack_kernel(cj, lv, where, packed, out):
    ntiles = out.shape[1] // TILE
    labels, ranks = tile_ranks(lv, ntiles)
    want = lv[where[1]] ^ cj[where[0]]
    for v in range(ntiles):
        block = packed[:, pl.ds(pl.multiple_of(ranks[v] * TILE, TILE), TILE)]
        keep = jnp.broadcast_to(labels[v] == want, block.shape)
        out[:, v * TILE:(v + 1) * TILE] = jnp.where(keep, block, jnp.zeros_like(block))


def kernel(dims, n_tile, n_red, pk, w_hbm, keep, out, wraw, wv, recv_h, recv_d, part_h, part_d, ybuf_h, ybuf_d, mine, theirs, mbuf,
           w_sem, send_sem, recv_sem, own_sem, ysend_sem, yrecv_sem, msend_sem, mrecv_sem):
    xs, zs, cs = dims
    me, my = lax.axis_index("tile"), lax.axis_index("red")
    n_k, rows = pk.shape[2], pk.shape[3]
    width = wv.shape[1]
    half = zs // 2
    core, z, x = me % cs, (me // cs) % zs, me // (cs * zs)
    partner = (x * zs + (z + half) % zs) * cs + core
    w_copy = pltpu.make_async_copy(w_hbm, wraw, w_sem)
    w_copy.start()

    barrier = pltpu.get_barrier_semaphore()

    def greet(n, carry):
        pl.semaphore_signal(barrier, inc=1, device_id=(peer(me, n, dims), my), device_id_type=MESH)
        return carry

    def greet_red(n, carry):
        pl.semaphore_signal(barrier, inc=1, device_id=(me, (my + n) % n_red), device_id_type=MESH)
        return carry

    lax.fori_loop(1, n_tile, greet, 0)
    lax.fori_loop(1, n_red, greet_red, 0)

    def clear(n, carry):
        first = ((n // half) * zs + (z + half - 2 + core + n % half) % zs) * cs * rows
        where = pl.ds(pl.multiple_of(first, cs * rows), cs * rows)
        for i in range(HALVED):
            for k in range(n_k):
                recv_h[i, k, where, :] = jnp.zeros((cs * rows, 2 * TILE), recv_h.dtype)
        return carry

    lax.fori_loop(0, xs * half, clear, 0)
    pl.semaphore_wait(barrier, n_tile + n_red - 2)

    own_rows = pl.ds(pl.multiple_of(me * rows, rows), rows)
    own = []

    def step_h(n, carry, i):
        j = peer(me, n, dims)
        j_core, j_z, j_x = j % cs, (j // cs) % zs, j // (cs * zs)
        across = ((z - j_z + 2 - j_core + zs) % zs) // half
        to = (j_x * zs + (j_z + across * half) % zs) * cs + j_core
        pltpu.make_async_remote_copy(
            src_ref=pk.at[i, j],
            dst_ref=recv_h.at[i, :, own_rows, pl.ds(pl.multiple_of(across * TILE, TILE), TILE)],
            send_sem=send_sem.at[i],
            recv_sem=recv_sem.at[i],
            device_id=(to, my),
            device_id_type=MESH,
        ).start()
        return carry

    def step_d(n, carry, i):
        j = peer(me, n, dims)
        pltpu.make_async_remote_copy(
            src_ref=pk.at[i, j],
            dst_ref=recv_d.at[i - HALVED, :, own_rows, :],
            send_sem=send_sem.at[i],
            recv_sem=recv_sem.at[i],
            device_id=(j, my),
            device_id_type=MESH,
        ).start()
        return carry

    for i in range(CHUNKS):
        if i < HALVED:
            lax.fori_loop(1, zs - 1, functools.partial(step_h, i=i), 0)
            lax.fori_loop(zs, n_tile, functools.partial(step_h, i=i), 0)
            copies = [
                pltpu.make_async_copy(pk.at[i, me], recv_h.at[i, :, own_rows, pl.ds(0, TILE)], own_sem.at[i, 0]),
                pltpu.make_async_copy(pk.at[i, partner], recv_h.at[i, :, own_rows, pl.ds(TILE, TILE)], own_sem.at[i, 1]),
            ]
        else:
            lax.fori_loop(1, n_tile, functools.partial(step_d, i=i), 0)
            copies = [pltpu.make_async_copy(pk.at[i, me], recv_d.at[i - HALVED, :, own_rows, :], own_sem.at[i, 0])]
        for copy in copies:
            copy.start()
        own.append(copies)

    w_copy.wait()
    row = lax.broadcasted_iota(jnp.int32, (TILE, n_k * TILE), 0)
    col = lax.broadcasted_iota(jnp.int32, (TILE, n_k * TILE), 1)
    picks = [jnp.where(col == n_k * row + k, 1.0, 0.0).astype(wv.dtype) for k in range(n_k)]

    def arrange(a, carry):
        a_rows = pl.ds(pl.multiple_of(a * TILE, TILE), TILE)
        pairs = wraw[a_rows].reshape(n_k * TILE, width)
        for k in range(n_k):
            plane = jnp.dot(picks[k], pairs, preferred_element_type=jnp.float32)
            wv[k, a_rows, :] = (plane * keep[a, k:k + 1, :]).astype(wv.dtype)
        return carry

    lax.fori_loop(0, n_red, arrange, 0)

    def multiply(i):
        for copy in own[i]:
            copy.wait()
        if i < HALVED:
            got, part, ybuf, at, n_got = recv_h, part_h, ybuf_h, i, n_tile - 2
        else:
            got, part, ybuf, at, n_got = recv_d, part_d, ybuf_d, i - HALVED, n_tile - 1
        others = got.at[at, :, pl.ds(0, n_got * rows), pl.ds(0, TILE)]
        pltpu.make_async_copy(others, others, recv_sem.at[i]).wait()

        def block(n, carry):
            to = (my + n) % n_red
            a_rows = pl.ds(pl.multiple_of(to * TILE, TILE), TILE)
            acc = jnp.dot(wv[0, a_rows, :], got[at, 0], preferred_element_type=jnp.float32)
            for k in range(1, n_k):
                acc += jnp.dot(wv[k, a_rows, :], got[at, k], preferred_element_type=jnp.float32)
            part[at, to] = acc.astype(part.dtype)

            @pl.when(n < n_red)
            def _():
                pltpu.make_async_remote_copy(
                    src_ref=part.at[at, to],
                    dst_ref=ybuf.at[at, my],
                    send_sem=ysend_sem.at[i],
                    recv_sem=yrecv_sem.at[i],
                    device_id=(me, to),
                    device_id_type=MESH,
                ).start()
            return carry

        lax.fori_loop(1, n_red + 1, block, 0)

    def add_up(i):
        part, ybuf, at = (part_h, ybuf_h, i) if i < HALVED else (part_d, ybuf_d, i - HALVED)
        others = ybuf.at[at, pl.ds(0, n_red - 1)]
        pltpu.make_async_copy(others, others, yrecv_sem.at[i]).wait()
        total = part[at, my].astype(jnp.float32)
        for d in range(1, n_red):
            total += ybuf[at, (my + d) % n_red].astype(jnp.float32)
        return total

    crossing = []

    def cross(i):
        total = add_up(i)
        mine[i] = total[:, :TILE]
        theirs[i] = total[:, TILE:].astype(theirs.dtype)
        copy = pltpu.make_async_remote_copy(
            src_ref=theirs.at[i], dst_ref=mbuf.at[i], send_sem=msend_sem.at[i], recv_sem=mrecv_sem.at[i],
            device_id=(partner, my), device_id_type=MESH)
        copy.start()
        crossing.append(copy)

    def finish(i):
        if i < HALVED:
            crossing[i].wait_recv()
            total = mine[i] + mbuf[i].astype(jnp.float32)
        else:
            total = add_up(i)
        out[:, i * TILE:(i + 1) * TILE] = total.astype(out.dtype)

    for kind, i in ORDER:
        {"multiply": multiply, "cross": cross, "finish": finish}[kind](i)

    for i in range(CHUNKS):
        at = i if i < HALVED else i - HALVED
        sent = pk.at[i, pl.ds(0, n_tile - 2 if i < HALVED else n_tile - 1)]
        pltpu.make_async_copy(sent, sent, send_sem.at[i]).wait()
        sent = (part_h if i < HALVED else part_d).at[at, pl.ds(0, n_red - 1)]
        pltpu.make_async_copy(sent, sent, ysend_sem.at[i]).wait()
    for copy in crossing:
        copy.wait_send()


def local(n_tile, n_red, amplitudes, intermediate, contract_irrep, column_irrep, virtual_irrep):
    n_k, n_j, rows, width = amplitudes.shape
    me, my = lax.axis_index("tile"), lax.axis_index("red")
    dims = (4, 8, 2) if n_tile == 64 else (1, n_tile // 2, 2)
    cw = SLOTS // CHUNKS * TILE
    bf = jnp.bfloat16
    smem = pl.BlockSpec(memory_space=pltpu.SMEM)
    hbm = pl.BlockSpec(memory_space=pl.ANY)
    vmem = pl.BlockSpec(memory_space=pltpu.VMEM)

    group = 8
    ntiles = width // TILE
    packed, keep = pl.pallas_call(
        pack_kernel,
        out_shape=(jax.ShapeDtypeStruct((CHUNKS, n_j, n_k, rows, cw), bf),
                   jax.ShapeDtypeStruct((ntiles, n_k, width), jnp.float32)),
        grid=(n_j // group,),
        in_specs=[smem, smem, smem, smem, pl.BlockSpec((n_k, group, rows, width), lambda g: (0, g, 0, 0))],
        out_specs=(pl.BlockSpec((CHUNKS, group, n_k, rows, cw), lambda g: (0, g, 0, 0, 0)),
                   pl.BlockSpec((ntiles, n_k, width), lambda g: (0, 0, 0))),
        scratch_shapes=[pltpu.SMEM((4 * SLOTS,), jnp.int32)],
    )(contract_irrep, column_irrep, virtual_irrep, jnp.reshape(me * rows // TILE, (1,)), amplitudes)

    summed = pl.pallas_call(
        functools.partial(kernel, dims, n_tile, n_red),
        out_shape=jax.ShapeDtypeStruct((TILE, SLOTS * TILE), bf),
        in_specs=[hbm, hbm, vmem],
        out_specs=vmem,
        scratch_shapes=[
            pltpu.VMEM((width, n_k, width), bf),
            pltpu.VMEM((n_k, width, width), bf),
            pltpu.VMEM((HALVED, n_k, width, 2 * TILE), bf),
            pltpu.VMEM((CHUNKS - HALVED, n_k, width, TILE), bf),
            pltpu.VMEM((HALVED, n_red, TILE, 2 * TILE), bf),
            pltpu.VMEM((CHUNKS - HALVED, n_red, TILE, TILE), bf),
            pltpu.VMEM((HALVED, n_red, TILE, 2 * TILE), bf),
            pltpu.VMEM((CHUNKS - HALVED, n_red, TILE, TILE), bf),
            pltpu.VMEM((HALVED, TILE, TILE), jnp.float32),
            pltpu.VMEM((HALVED, TILE, TILE), bf),
            pltpu.VMEM((HALVED, TILE, TILE), bf),
            pltpu.SemaphoreType.DMA,
            pltpu.SemaphoreType.DMA((CHUNKS,)),
            pltpu.SemaphoreType.DMA((CHUNKS,)),
            pltpu.SemaphoreType.DMA((CHUNKS, 2)),
            pltpu.SemaphoreType.DMA((CHUNKS,)),
            pltpu.SemaphoreType.DMA((CHUNKS,)),
            pltpu.SemaphoreType.DMA((HALVED,)),
            pltpu.SemaphoreType.DMA((HALVED,)),
        ],
        compiler_params=pltpu.CompilerParams(
            collective_id=0, has_side_effects=True, vmem_limit_bytes=48 * 2**20
        ),
        cost_estimate=pl.CostEstimate(flops=2 * width**2 * n_k * SLOTS * TILE, bytes_accessed=9 * 2**20,
                                      transcendentals=0),
    )(packed, intermediate, keep)

    out = pl.pallas_call(
        unpack_kernel,
        out_shape=jax.ShapeDtypeStruct((TILE, width), bf),
        in_specs=[smem, smem, smem, vmem],
        out_specs=vmem,
    )(column_irrep, virtual_irrep, jnp.stack([me, my]), summed)
    return out[:, None, :]


def solution(mesh):
    in_specs = (P("red", None, "tile", None), P(None, "red", None), P("red"), P(), P())
    out_specs = P("red", "tile", None)
    body = functools.partial(local, mesh.shape["tile"], mesh.shape["red"])
    return jax.shard_map(body, mesh=mesh, in_specs=in_specs, out_specs=out_specs, check_vma=False)
```

time: 98.9 us -> 82 us (0.83)
  other arithmetic: 9.51 us -> 0.64 us
  Pallas kernels: 84.2 us -> 77.9 us
  local copies, waits for them, and re-layouts: 4.74 us -> 3.07 us
    select_n x1 -> x0, other arithmetic: 8.02 us -> none  [local(): jnp.where(label == 0, intermediate, jnp.zeros_like(intermediate))]
    pallas_call x1, Pallas kernels: 75.6 us -> 69.3 us  [local(): pl.pallas_call(functools.partial(kernel, dims, n_tile, n_red), out_shape=...]
    unnamed x5 -> x6, local copies, waits for them, and re-layouts: 4.02 us -> 3.07 us
where the time goes in v2:
time: 82 us; the launch traced here: 81.7 us
  Pallas kernels  77.9 us (95%)
  local copies, waits for them, and re-layouts  3.07 us (4%)
    pallas_call x1, Pallas kernels, local(): pl.pallas_call(functools.partial(kernel, dims, n_tile, n_red), out_shape=...  69.3 us
    pallas_call x1, Pallas kernels, local(): pl.pallas_call(pack_kernel, out_shape=(jax.ShapeDtypeStruct((CHUNKS, n_j,...  6.96 us
    unnamed x6, local copies, waits for them, and re-layouts  3.07 us
    pallas_call x1, Pallas kernels, local(): pl.pallas_call(unpack_kernel, out_shape=jax.ShapeDtypeStruct((TILE, width...  1.71 us

profile of v2, /device:TPU:1, one launch (start us, length us, event | category | flops | bytes accessed | tf_op | source)
XLA Modules:
  0.0 81.7 jit_solution(16305114695579928394)
XLA Ops:
  0.0 0.6 pad_add_fusion.where
  0.6 7.0 %shard_map.55 = (bf16[4,64,2,16,128]{4,3,2,1,0:T(8,128)(2,1)}, f32[8,2,1024]{2,1,0:T(2,128)}) custom-call(s32[2]{0:T(128)} %ck.1, s32[64]{0:T(128)} %cj.3, s32[8]{0:T(128)} %lv.3, s32[1]{0:T(128)} %bitcast.2.where, bf16[2,64,16,1024]{3,2,1,0:T(8,128)(2,1)} %t.1), custom_call_target="tpu_custom_call" | custom-call | tf_op jit(solution)/shard_map/pallas_call | solution.py:267
  7.6 0.0 copy-start.1
  7.6 1.6 %copy-done.1 = bf16[4,64,2,16,128]{4,3,2,1,0:T(8,128)(2,1)S(1)} copy-done((bf16[4,64,2,16,128]{4,3,2,1,0:T(8,128)(2,1)S(1)}, bf16[4,64,2,16,128]{4,3,2,1,0:T(8,128)(2,1)}, u32[]{:S(2)}) %copy-start.1) | copy-done | bytes 2097176
  9.2 0.0 copy-start.2
  9.2 0.8 %copy-done.2 = f32[8,2,1024]{2,1,0:T(2,128)S(1)} copy-done((f32[8,2,1024]{2,1,0:T(2,128)S(1)}, f32[8,2,1024]{2,1,0:T(2,128)}, u32[]{:S(2)}) %copy-start.2) | copy-done | bytes 65560
  10.0 69.3 %shard_map.56.packed = bf16[128,512]{1,0:T(8,128)(2,1)S(1)} custom-call(bf16[4,64,2,16,128]{4,3,2,1,0:T(8,128)(2,1)S(1)} %copy-done.1, bf16[1024,2,1024]{2,1,0:T(2,128)(2,1)} %w_hbm.1, f32[8,2,1024]{2,1,0:T(2,128)S(1)} %copy-done.2), custom_call_target="tpu_custom_call" | custom-call | flops 2147483648 | bytes 9437184 | tf_op jit(solution)/shard_map/pallas_call | solution.py:278
  79.3 0.0 copy-start
  79.3 0.6 copy-done
  80.0 1.7 %shard_map.57 = bf16[128,1024]{1,0:T(8,128)(2,1)} custom-call(s32[64]{0:T(128)} %cj.3, s32[8]{0:T(128)} %lv.3, s32[2]{0:T(128)} %pad_add_fusion.where, bf16[128,512]{1,0:T(8,128)(2,1)} %copy-done), custom_call_target="tpu_custom_call" | custom-call | tf_op jit(solution)/shard_map/pallas_call | solution.py:311
Async XLA Ops:
  7.6 1.6 %copy-start.1 = (bf16[4,64,2,16,128]{4,3,2,1,0:T(8,128)(2,1)S(1)}, bf16[4,64,2,16,128]{4,3,2,1,0:T(8,128)(2,1)}, u32[]{:S(2)}) copy-start(bf16[4,64,2,16,128]{4,3,2,1,0:T(8,128)(2,1)} %get-tuple-element.7.pk) | copy-start | bytes 6291460
  9.2 0.8 %copy-start.2 = (f32[8,2,1024]{2,1,0:T(2,128)S(1)}, f32[8,2,1024]{2,1,0:T(2,128)}, u32[]{:S(2)}) copy-start(f32[8,2,1024]{2,1,0:T(2,128)} %get-tuple-element.8.keep) | copy-start | bytes 196612
  79.3 0.6 copy-start

commit v3 on v0

v3 whole, which is shorter than its diff:
```python
import functools

import jax
import jax.numpy as jnp
from jax import lax
from jax.experimental import pallas as pl
from jax.experimental.pallas import tpu as pltpu
from jax.sharding import PartitionSpec as P

TILE = 128
SLOTS = 4
HALVED = (0, 1, 2)
RING = (0, 1, 2)
ORDER = (
    ("multiply", 0), ("ring", 0, 2), ("multiply", 1), ("ring", 0, 3), ("ring", 1, 2),
    ("ring", 0, 4), ("multiply", 2), ("ring", 1, 3), ("cross", 0), ("ring", 2, 2),
    ("ring", 1, 4), ("ring", 2, 3), ("cross", 1), ("ring", 2, 4), ("cross", 2),
    ("multiply", 3), ("finish", 0), ("finish", 1), ("finish", 2), ("finish", 3),
)
MESH = pl.DeviceIdType.MESH


def wrap(value, size):
    return jnp.where(value >= size, value - size, value)


def tile_codes(lv, ntiles):
    codes = []
    for v in range(ntiles):
        code = lv[v] * 8
        for u in range(v):
            code = code + (lv[u] == lv[v]).astype(jnp.int32)
        codes.append(code)
    return codes


def kernel(dims, n_tile, n_red, ck, cj, lv, t_hbm, w_hbm, out, tv, wraw, wv, lanes, pk, recv, part, ybuf, mine, theirs, mbuf, sums,
           t_sem, w_sem, send_sem, recv_sem, own_sem, ysend_sem, yrecv_sem, msend_sem, mrecv_sem):
    xs, zs, cs = dims
    me, my = lax.axis_index("tile"), lax.axis_index("red")
    n_k, n_j, rows, width = tv.shape
    ntiles = width // TILE
    half, halfway = zs // 2, n_red // 2
    core, z, x = me % cs, (me // cs) % zs, me // (cs * zs)
    partner = (x * zs + wrap(z + half, zs)) * cs + core

    steps = [(dcore, dz) for dcore in range(cs) for dz in (0, 1, zs - 1, 2, zs - 2, 3, zs - 3, half)]
    places, homes = [], []
    for dcore, dz in steps:
        j_core, j_z = wrap(core + dcore, cs), wrap(z + dz, zs)
        behind = wrap(zs - dz + 2 - j_core, zs)
        across = jnp.where(behind >= half, 1, 0)
        places.append(j_z * cs + j_core)
        homes.append((wrap(j_z + half * across, zs) * cs + j_core, across))

    def each_peer(visit, skip):
        for q in range(len(steps)):
            if steps[q] not in skip:
                visit(x * zs * cs, q)

        def plane(dx, carry):
            for q in range(len(steps)):
                visit(wrap(x + dx, xs) * zs * cs, q)
            return carry

        lax.fori_loop(1, xs, plane, 0)

    t_copy = pltpu.make_async_copy(t_hbm, tv, t_sem)
    t_copy.start()
    w_copy = pltpu.make_async_copy(w_hbm, wraw, w_sem)
    w_copy.start()

    barrier = pltpu.get_barrier_semaphore()

    def greet(base, q):
        pl.semaphore_signal(barrier, inc=1, device_id=(base + places[q], my), device_id_type=MESH)

    each_peer(greet, [(0, 0)])
    for d in range(1, n_red):
        pl.semaphore_signal(barrier, inc=1, device_id=(me, wrap(my + d, n_red)), device_id_type=MESH)

    def clear(n, carry):
        for far in range(half):
            first = (n * zs + wrap(z + wrap(half - 2 + core + far, zs), zs)) * cs * rows
            where = pl.ds(pl.multiple_of(first, cs * rows), cs * rows)
            for i in HALVED:
                for k in range(n_k):
                    recv[i][k, where, :] = jnp.zeros((cs * rows, 2 * TILE), recv[i].dtype)
        return carry

    lax.fori_loop(0, xs, clear, 0)

    codes = tile_codes(lv, ntiles)
    own_label = lv[me * rows // TILE]
    for c in range(ntiles):
        lanes[:, c * TILE:(c + 1) * TILE] = jnp.full((8, TILE), lv[c], jnp.int32)
    t_copy.wait()

    def pack(j, carry):
        for k in range(n_k):
            key = jnp.full((rows, TILE), (ck[k] ^ cj[j] ^ own_label) * 8, jnp.int32)
            tiles = [tv[k, j, :, v * TILE:(v + 1) * TILE].astype(jnp.float32) for v in range(ntiles)]
            for i in range(SLOTS):
                found = tiles[i]
                for v in range(i + 1, ntiles):
                    found = jnp.where(key == codes[v] - i, tiles[v], found)
                pk[i, j, k] = found.astype(pk.dtype)
        return carry

    lax.fori_loop(0, n_j, pack, 0)
    pl.semaphore_wait(barrier, n_tile + n_red - 2)

    own_rows = pl.ds(pl.multiple_of(me * rows, rows), rows)
    own = []

    def send(i, base, q):
        place, (home, across) = places[q], homes[q]
        if i in HALVED:
            to = base + home
            columns = pl.ds(pl.multiple_of(across * TILE, TILE), TILE)
        else:
            to = base + place
            columns = pl.ds(0, TILE)
        pltpu.make_async_remote_copy(
            src_ref=pk.at[i, base + place],
            dst_ref=recv[i].at[:, own_rows, columns],
            send_sem=send_sem.at[i],
            recv_sem=recv_sem.at[i],
            device_id=(to, my),
            device_id_type=MESH,
        ).start()

    for i in range(SLOTS):
        copies = [pltpu.make_async_copy(pk.at[i, me], recv[i].at[:, own_rows, pl.ds(0, TILE)], own_sem.at[i, 0])]
        if i in HALVED:
            each_peer(functools.partial(send, i), [(0, 0), (0, half)])
            copies.append(pltpu.make_async_copy(
                pk.at[i, partner], recv[i].at[:, own_rows, pl.ds(TILE, TILE)], own_sem.at[i, 1]))
        else:
            each_peer(functools.partial(send, i), [(0, 0)])
        for copy in copies:
            copy.start()
        own.append(copies)

    w_copy.wait()
    row = lax.broadcasted_iota(jnp.int32, (TILE, n_k * TILE), 0)
    col = lax.broadcasted_iota(jnp.int32, (TILE, n_k * TILE), 1)
    picks = [jnp.where(col == n_k * row + k, 1.0, 0.0).astype(wv.dtype) for k in range(n_k)]

    def arrange(a, carry):
        a_rows = pl.ds(pl.multiple_of(a * TILE, TILE), TILE)
        pairs = wraw[a_rows].reshape(n_k * TILE, width)
        for k in range(n_k):
            plane = jnp.dot(picks[k], pairs, preferred_element_type=jnp.float32)
            keep = jnp.broadcast_to(lanes[0:1, :], plane.shape) == jnp.full(plane.shape, lv[a] ^ ck[k], jnp.int32)
            wv[k, a_rows, :] = jnp.where(keep, plane, 0.0).astype(wv.dtype)
        return carry

    lax.fori_loop(0, ntiles, arrange, 0)

    def around(i, direction, t, block):
        return pltpu.make_async_remote_copy(
            src_ref=block,
            dst_ref=ybuf[i].at[direction * halfway + t - 1],
            send_sem=ysend_sem.at[i, direction * halfway + t - 1],
            recv_sem=yrecv_sem.at[i, direction * halfway + t - 1],
            device_id=(me, wrap(my + (1 if direction == 0 else n_red - 1), n_red)),
            device_id_type=MESH,
        )

    ring_copies = {}
    first_pair = wrap(my // 2 + n_red // 4, n_red // 2)

    def multiply(i):
        for copy in own[i]:
            copy.wait()
        n_got = n_tile - 2 if i in HALVED else n_tile - 1
        others = recv[i].at[:, pl.ds(0, n_got * rows), pl.ds(0, TILE)]
        pltpu.make_async_copy(others, others, recv_sem.at[i]).wait()

        def block(n, carry):
            pair = wrap(first_pair + n, n_red // 2)
            a_rows = pl.ds(pl.multiple_of(pair * 2 * TILE, 2 * TILE), 2 * TILE)
            acc = jnp.dot(wv[0, a_rows, :], recv[i][0], preferred_element_type=jnp.float32)
            for k in range(1, n_k):
                acc += jnp.dot(wv[k, a_rows, :], recv[i][k], preferred_element_type=jnp.float32)
            for h in range(2):
                to = pair * 2 + h
                part[i][to] = acc[h * TILE:(h + 1) * TILE].astype(part[i].dtype)

                if i not in RING:
                    @pl.when(to != my)
                    def _():
                        pltpu.make_async_remote_copy(
                            src_ref=part[i].at[to],
                            dst_ref=ybuf[i].at[my],
                            send_sem=ysend_sem.at[i, 0],
                            recv_sem=yrecv_sem.at[i, 0],
                            device_id=(me, to),
                            device_id_type=MESH,
                        ).start()
            return carry

        lax.fori_loop(0, n_red // 2, block, 0)
        if i in RING:
            ring_copies[i, 0, 1] = around(i, 0, 1, part[i].at[wrap(my + halfway, n_red)])
            ring_copies[i, 1, 1] = around(i, 1, 1, part[i].at[wrap(my + halfway + 1, n_red)])
            ring_copies[i, 0, 1].start()
            ring_copies[i, 1, 1].start()

    def ring(i, t):
        for direction in (0, 1):
            if direction == 1 and t == halfway:
                continue
            ring_copies[i, direction, t - 1].wait_recv()
            at = direction * halfway + t - 2
            ahead = (halfway + 1 - t) if direction == 0 else (n_red - halfway + t)
            total = part[i][wrap(my + ahead, n_red)].astype(jnp.float32) + ybuf[i][at].astype(jnp.float32)
            sums[i][at] = total.astype(sums[i].dtype)
            copy = around(i, direction, t, sums[i].at[at])
            copy.start()
            ring_copies[i, direction, t] = copy

    def add_up(i):
        total = part[i][my].astype(jnp.float32)
        if i in RING:
            ring_copies[i, 0, halfway].wait_recv()
            ring_copies[i, 1, halfway - 1].wait_recv()
            total += ybuf[i][halfway - 1].astype(jnp.float32)
            total += ybuf[i][2 * halfway - 2].astype(jnp.float32)
        else:
            others = ybuf[i].at[pl.ds(0, n_red - 1)]
            pltpu.make_async_copy(others, others, yrecv_sem.at[i, 0]).wait()
            for d in range(1, n_red):
                total += ybuf[i][wrap(my + d, n_red)].astype(jnp.float32)
        return total

    crossing = {}

    def cross(i):
        total = add_up(i)
        mine[i] = total[:, :TILE]
        theirs[i] = total[:, TILE:].astype(theirs.dtype)
        copy = pltpu.make_async_remote_copy(
            src_ref=theirs.at[i], dst_ref=mbuf.at[i], send_sem=msend_sem.at[i], recv_sem=mrecv_sem.at[i],
            device_id=(partner, my), device_id_type=MESH)
        copy.start()
        crossing[i] = copy

    def finish(i):
        if i in HALVED:
            crossing[i].wait_recv()
            mine[i] += mbuf[i].astype(jnp.float32)
        else:
            mine[i] = add_up(i)

    for kind, *where in ORDER:
        {"multiply": multiply, "ring": ring, "cross": cross, "finish": finish}[kind](*where)

    want = jnp.full((TILE, TILE), (lv[my] ^ cj[me]) * 8, jnp.int32)
    for v in range(ntiles):
        found = jnp.zeros((TILE, TILE), jnp.float32)
        for i in range(min(v + 1, SLOTS)):
            found = jnp.where(want == codes[v] - i, mine[i], found)
        out[:, v * TILE:(v + 1) * TILE] = found.astype(out.dtype)

    for i in range(SLOTS):
        sent = pk.at[i, pl.ds(0, n_tile - 2 if i in HALVED else n_tile - 1)]
        pltpu.make_async_copy(sent, sent, send_sem.at[i]).wait()
        if i not in RING:
            sent = part[i].at[pl.ds(0, n_red - 1)]
            pltpu.make_async_copy(sent, sent, ysend_sem.at[i, 0]).wait()
    for copy in list(ring_copies.values()) + list(crossing.values()):
        copy.wait_send()


def local(n_tile, n_red, amplitudes, intermediate, contract_irrep, column_irrep, virtual_irrep):
    n_k, n_j, rows, width = amplitudes.shape
    dims = (4, 8, 2)
    bf = jnp.bfloat16
    smem = pl.BlockSpec(memory_space=pltpu.SMEM)
    hbm = pl.BlockSpec(memory_space=pl.ANY)
    cols = [2 * TILE if i in HALVED else TILE for i in range(SLOTS)]
    blocks = [pltpu.VMEM((n_red, TILE, c), bf) for c in cols]
    out = pl.pallas_call(
        functools.partial(kernel, dims, n_tile, n_red),
        out_shape=jax.ShapeDtypeStruct((TILE, width), bf),
        in_specs=[smem, smem, smem, hbm, hbm],
        out_specs=pl.BlockSpec(memory_space=pltpu.VMEM),
        scratch_shapes=[
            pltpu.VMEM((n_k, n_j, rows, width), bf),
            pltpu.VMEM((width, n_k, width), bf),
            pltpu.VMEM((n_k, width, width), bf),
            pltpu.VMEM((8, width), jnp.int32),
            pltpu.VMEM((SLOTS, n_j, n_k, rows, TILE), bf),
            [pltpu.VMEM((n_k, width, c), bf) for c in cols],
            blocks,
            blocks,
            pltpu.VMEM((SLOTS, TILE, TILE), jnp.float32),
            pltpu.VMEM((SLOTS, TILE, TILE), bf),
            pltpu.VMEM((SLOTS, TILE, TILE), bf),
            blocks,
            pltpu.SemaphoreType.DMA,
            pltpu.SemaphoreType.DMA,
            pltpu.SemaphoreType.DMA((SLOTS,)),
            pltpu.SemaphoreType.DMA((SLOTS,)),
            pltpu.SemaphoreType.DMA((SLOTS, 2)),
            pltpu.SemaphoreType.DMA((SLOTS, n_red)),
            pltpu.SemaphoreType.DMA((SLOTS, n_red)),
            pltpu.SemaphoreType.DMA((SLOTS,)),
            pltpu.SemaphoreType.DMA((SLOTS,)),
        ],
        compiler_params=pltpu.CompilerParams(
            collective_id=0, has_side_effects=True, vmem_limit_bytes=48 * 2**20
        ),
        cost_estimate=pl.CostEstimate(flops=2 * width**2 * n_k * SLOTS * TILE, bytes_accessed=9 * 2**20,
                                      transcendentals=0),
    )(contract_irrep, column_irrep, virtual_irrep, amplitudes, intermediate)
    return out[:, None, :]


def solution(mesh):
    in_specs = (P("red", None, "tile", None), P(None, "red", None), P("red"), P(), P())
    out_specs = P("red", "tile", None)
    body = functools.partial(local, mesh.shape["tile"], mesh.shape["red"])
    return jax.shard_map(body, mesh=mesh, in_specs=in_specs, out_specs=out_specs, check_vma=False)
```

time: 181 us -> 68.6 us (0.38)
  the two profiles are of different devices: /device:TPU:1 before, /device:TPU:4 now
where the time goes in v3:
time: 68.6 us; the launch traced here: 68.4 us
  Pallas kernels  63.6 us (93%)
  local copies, waits for them, and re-layouts  4.86 us (7%)
    pallas_call x1, Pallas kernels, local(): pl.pallas_call(functools.partial(kernel, dims, n_tile, n_red), out_shape=...  63.6 us
    unnamed x9, local copies, waits for them, and re-layouts  4.86 us

profile of v3, /device:TPU:4, one launch (start us, length us, event | category | flops | bytes accessed | tf_op | source)
XLA Modules:
  0.0 68.4 jit_solution(1661590303832381863)
XLA Ops:
  0.0 0.0 copy-start
  0.0 2.2 %copy-done = bf16[2,64,16,1024]{3,2,1,0:T(8,128)(2,1)S(1)} copy-done((bf16[2,64,16,1024]{3,2,1,0:T(8,128)(2,1)S(1)}, bf16[2,64,16,1024]{3,2,1,0:T(8,128)(2,1)}, u32[]{:S(2)}) %copy-start) | copy-done | bytes 4194328
  2.2 0.0 copy-start.1
  2.2 0.7 copy-done.1
  2.8 0.0 copy-start.2
  2.8 0.7 copy-done.2
  3.5 0.0 copy-start.3
  3.5 0.7 copy-done.3
  4.2 63.6 %shard_map.55 = bf16[128,1024]{1,0:T(8,128)(2,1)S(1)} custom-call(s32[2]{0:T(128)S(1)} %copy-done.1, s32[64]{0:T(128)S(1)} %copy-done.2, s32[8]{0:T(128)S(1)} %copy-done.3, bf16[2,64,16,1024]{3,2,1,0:T(8,128)(2,1)S(1)} %copy-done, bf16[1024,2,1024]{2,1,0:T(2,128)(2,1)} %w_hbm.1), custom_call_target="tpu_custom_call" | custom-call | flops 2147483648 | bytes 9437184 | tf_op jit(solution)/shard_map/pallas_call | solution.py:285
  67.7 0.7 %copy.7 = bf16[128,1,1024]{2,0,1:T(8,128)(2,1)} copy(bf16[128,1,1024]{2,0,1:T(8,128)(2,1)S(1)} %bitcast.1) | data formatting | bytes 524288
Async XLA Ops:
  0.0 2.2 %copy-start = (bf16[2,64,16,1024]{3,2,1,0:T(8,128)(2,1)S(1)}, bf16[2,64,16,1024]{3,2,1,0:T(8,128)(2,1)}, u32[]{:S(2)}) copy-start(bf16[2,64,16,1024]{3,2,1,0:T(8,128)(2,1)} %t_hbm.1) | copy-start | bytes 12582916
  2.2 0.7 copy-start.1
  2.8 0.7 copy-start.2
  3.5 0.7 copy-start.3

commit v4 on v3

--- a/solution.py
+++ b/solution.py
@@ -10,12 +10,12 @@
 TILE = 128
 SLOTS = 4
 HALVED = (0, 1, 2)
-RING = (0, 1, 2)
+TWO_STEP = (0, 1, 2, 3)
 ORDER = (
-    ("multiply", 0), ("ring", 0, 2), ("multiply", 1), ("ring", 0, 3), ("ring", 1, 2),
-    ("ring", 0, 4), ("multiply", 2), ("ring", 1, 3), ("cross", 0), ("ring", 2, 2),
-    ("ring", 1, 4), ("ring", 2, 3), ("cross", 1), ("ring", 2, 4), ("cross", 2),
-    ("multiply", 3), ("finish", 0), ("finish", 1), ("finish", 2), ("finish", 3),
+    ("launch", 0), ("launch", 1), ("launch", 2), ("launch", 3), ("weights",),
+    ("multiply", 0), ("combine", 0), ("multiply", 1), ("combine", 1), ("cross", 0),
+    ("multiply", 2), ("combine", 2), ("cross", 1), ("multiply", 3), ("cross", 2),
+    ("combine", 3), ("finish", 0), ("finish", 1), ("finish", 2), ("finish", 3),
 )
 MESH = pl.DeviceIdType.MESH
 
@@ -40,7 +40,7 @@
     me, my = lax.axis_index("tile"), lax.axis_index("red")
     n_k, n_j, rows, width = tv.shape
     ntiles = width // TILE
-    half, halfway = zs // 2, n_red // 2
+    half = zs // 2
     core, z, x = me % cs, (me // cs) % zs, me // (cs * zs)
     partner = (x * zs + wrap(z + half, zs)) * cs + core
 
@@ -111,7 +111,7 @@
     pl.semaphore_wait(barrier, n_tile + n_red - 2)
 
     own_rows = pl.ds(pl.multiple_of(me * rows, rows), rows)
-    own = []
+    own = {}
 
     def send(i, base, q):
         place, (home, across) = places[q], homes[q]
@@ -130,7 +130,7 @@
             device_id_type=MESH,
         ).start()
 
-    for i in range(SLOTS):
+    def launch(i):
         copies = [pltpu.make_async_copy(pk.at[i, me], recv[i].at[:, own_rows, pl.ds(0, TILE)], own_sem.at[i, 0])]
         if i in HALVED:
             each_peer(functools.partial(send, i), [(0, 0), (0, half)])
@@ -140,35 +140,42 @@
             each_peer(functools.partial(send, i), [(0, 0)])
         for copy in copies:
             copy.start()
-        own.append(copies)
-
-    w_copy.wait()
-    row = lax.broadcasted_iota(jnp.int32, (TILE, n_k * TILE), 0)
-    col = lax.broadcasted_iota(jnp.int32, (TILE, n_k * TILE), 1)
-    picks = [jnp.where(col == n_k * row + k, 1.0, 0.0).astype(wv.dtype) for k in range(n_k)]
-
-    def arrange(a, carry):
-        a_rows = pl.ds(pl.multiple_of(a * TILE, TILE), TILE)
-        pairs = wraw[a_rows].reshape(n_k * TILE, width)
-        for k in range(n_k):
-            plane = jnp.dot(picks[k], pairs, preferred_element_type=jnp.float32)
-            keep = jnp.broadcast_to(lanes[0:1, :], plane.shape) == jnp.full(plane.shape, lv[a] ^ ck[k], jnp.int32)
-            wv[k, a_rows, :] = jnp.where(keep, plane, 0.0).astype(wv.dtype)
-        return carry
-
-    lax.fori_loop(0, ntiles, arrange, 0)
-
-    def around(i, direction, t, block):
+        own[i] = copies
+
+    def weights():
+        w_copy.wait()
+        row = lax.broadcasted_iota(jnp.int32, (TILE, n_k * TILE), 0)
+        col = lax.broadcasted_iota(jnp.int32, (TILE, n_k * TILE), 1)
+        picks = [jnp.where(col == n_k * row + k, 1.0, 0.0).astype(wv.dtype) for k in range(n_k)]
+
+        def arrange(a, carry):
+            a_rows = pl.ds(pl.multiple_of(a * TILE, TILE), TILE)
+            pairs = wraw[a_rows].reshape(n_k * TILE, width)
+            for k in range(n_k):
+                plane = jnp.dot(picks[k], pairs, preferred_element_type=jnp.float32)
+                keep = jnp.broadcast_to(lanes[0:1, :], plane.shape) == jnp.full(plane.shape, lv[a] ^ ck[k], jnp.int32)
+                wv[k, a_rows, :] = jnp.where(keep, plane, 0.0).astype(wv.dtype)
+            return carry
+
+        lax.fori_loop(0, ntiles, arrange, 0)
+
+    def along(offset):
+        offset = offset % n_red
+        return wrap(my + jnp.where(core == 1, n_red - offset, offset), n_red)
+
+    first_step = ((0, -3, -1), (1, 4, 2), (2, 3, 1), (3, -1, -1), (4, 1, 1))
+
+    def hop(i, slot, block, offset):
         return pltpu.make_async_remote_copy(
             src_ref=block,
-            dst_ref=ybuf[i].at[direction * halfway + t - 1],
-            send_sem=ysend_sem.at[i, direction * halfway + t - 1],
-            recv_sem=yrecv_sem.at[i, direction * halfway + t - 1],
-            device_id=(me, wrap(my + (1 if direction == 0 else n_red - 1), n_red)),
+            dst_ref=ybuf[i].at[slot],
+            send_sem=ysend_sem.at[i, slot],
+            recv_sem=yrecv_sem.at[i, slot],
+            device_id=(me, along(offset)),
             device_id_type=MESH,
         )
 
-    ring_copies = {}
+    hops = {}
     first_pair = wrap(my // 2 + n_red // 4, n_red // 2)
 
     def multiply(i):
@@ -188,7 +195,7 @@
                 to = pair * 2 + h
                 part[i][to] = acc[h * TILE:(h + 1) * TILE].astype(part[i].dtype)
 
-                if i not in RING:
+                if i not in TWO_STEP:
                     @pl.when(to != my)
                     def _():
                         pltpu.make_async_remote_copy(
@@ -202,32 +209,27 @@
             return carry
 
         lax.fori_loop(0, n_red // 2, block, 0)
-        if i in RING:
-            ring_copies[i, 0, 1] = around(i, 0, 1, part[i].at[wrap(my + halfway, n_red)])
-            ring_copies[i, 1, 1] = around(i, 1, 1, part[i].at[wrap(my + halfway + 1, n_red)])
-            ring_copies[i, 0, 1].start()
-            ring_copies[i, 1, 1].start()
-
-    def ring(i, t):
-        for direction in (0, 1):
-            if direction == 1 and t == halfway:
-                continue
-            ring_copies[i, direction, t - 1].wait_recv()
-            at = direction * halfway + t - 2
-            ahead = (halfway + 1 - t) if direction == 0 else (n_red - halfway + t)
-            total = part[i][wrap(my + ahead, n_red)].astype(jnp.float32) + ybuf[i][at].astype(jnp.float32)
-            sums[i][at] = total.astype(sums[i].dtype)
-            copy = around(i, direction, t, sums[i].at[at])
-            copy.start()
-            ring_copies[i, direction, t] = copy
+        if i in TWO_STEP:
+            for slot, to, by in first_step:
+                hops[i, slot] = hop(i, slot, part[i].at[along(to)], by)
+                hops[i, slot].start()
+
+    def combine(i):
+        for slot, to, parts in ((5, -2, (0,)), (6, 2, (1, 2))):
+            total = part[i][along(to)].astype(jnp.float32)
+            for p in parts:
+                hops[i, p].wait_recv()
+                total += ybuf[i][p].astype(jnp.float32)
+            sums[i][slot] = total.astype(sums[i].dtype)
+            hops[i, slot] = hop(i, slot, sums[i].at[slot], to)
+            hops[i, slot].start()
 
     def add_up(i):
         total = part[i][my].astype(jnp.float32)
-        if i in RING:
-            ring_copies[i, 0, halfway].wait_recv()
-            ring_copies[i, 1, halfway - 1].wait_recv()
-            total += ybuf[i][halfway - 1].astype(jnp.float32)
-            total += ybuf[i][2 * halfway - 2].astype(jnp.float32)
+        if i in TWO_STEP:
+            for slot in (3, 4, 5, 6):
+                hops[i, slot].wait_recv()
+                total += ybuf[i][slot].astype(jnp.float32)
         else:
             others = ybuf[i].at[pl.ds(0, n_red - 1)]
             pltpu.make_async_copy(others, others, yrecv_sem.at[i, 0]).wait()
@@ -255,7 +257,7 @@
             mine[i] = add_up(i)
 
     for kind, *where in ORDER:
-        {"multiply": multiply, "ring": ring, "cross": cross, "finish": finish}[kind](*where)
+        {"launch": launch, "weights": weights, "multiply": multiply, "combine": combine, "cross": cross, "finish": finish}[kind](*where)
 
     want = jnp.full((TILE, TILE), (lv[my] ^ cj[me]) * 8, jnp.int32)
     for v in range(ntiles):
@@ -267,10 +269,10 @@
     for i in range(SLOTS):
         sent = pk.at[i, pl.ds(0, n_tile - 2 if i in HALVED else n_tile - 1)]
         pltpu.make_async_copy(sent, sent, send_sem.at[i]).wait()
-        if i not in RING:
+        if i not in TWO_STEP:
             sent = part[i].at[pl.ds(0, n_red - 1)]
             pltpu.make_async_copy(sent, sent, ysend_sem.at[i, 0]).wait()
-    for copy in list(ring_copies.values()) + list(crossing.values()):
+    for copy in list(hops.values()) + list(crossing.values()):
         copy.wait_send()
 
 
@@ -311,7 +313,7 @@
             pltpu.SemaphoreType.DMA((SLOTS,)),
         ],
         compiler_params=pltpu.CompilerParams(
-            collective_id=0, has_side_effects=True, vmem_limit_bytes=48 * 2**20
+            collective_id=0, has_side_effects=True, vmem_limit_bytes=59 * 2**20
         ),
         cost_estimate=pl.CostEstimate(flops=2 * width**2 * n_k * SLOTS * TILE, bytes_accessed=9 * 2**20,
                                       transcendentals=0),

time: 68.6 us -> 63 us (0.918)
  the two profiles are of different devices: /device:TPU:4 before, /device:TPU:1 now
where the time goes in v4:
time: 63 us; the launch traced here: 62.6 us
  Pallas kernels  61 us (97%)
  local copies, waits for them, and re-layouts  1.67 us (3%)
    pallas_call x1, Pallas kernels, local(): pl.pallas_call(functools.partial(kernel, dims, n_tile, n_red), out_shape=...  61 us
    unnamed x1, local copies, waits for them, and re-layouts  1.67 us

profile of v4, /device:TPU:1, one launch (start us, length us, event | category | flops | bytes accessed | tf_op | source)
XLA Modules:
  0.0 62.6 jit_solution(8542265340275432344)
XLA Ops:
  0.0 61.0 %shard_map.55 = bf16[128,1024]{1,0:T(8,128)(2,1)} custom-call(s32[2]{0:T(128)} %ck.1, s32[64]{0:T(128)} %cj.1, s32[8]{0:T(128)} %lv.1, bf16[2,64,16,1024]{3,2,1,0:T(8,128)(2,1)} %t_hbm.1, bf16[1024,2,1024]{2,1,0:T(2,128)(2,1)} %w_hbm.1), custom_call_target="tpu_custom_call" | custom-call | flops 2147483648 | bytes 9437184 | tf_op jit(solution)/shard_map/pallas_call | solution.py:287
  61.0 1.7 %copy.7 = bf16[128,1,1024]{2,0,1:T(8,128)(2,1)} copy(bf16[128,1,1024]{2,0,1:T(8,128)(2,1)} %bitcast.1) | data formatting | bytes 524288

commit v5 on v4

--- a/solution.py
+++ b/solution.py
@@ -44,7 +44,7 @@
     core, z, x = me % cs, (me // cs) % zs, me // (cs * zs)
     partner = (x * zs + wrap(z + half, zs)) * cs + core
 
-    steps = [(dcore, dz) for dcore in range(cs) for dz in (0, 1, zs - 1, 2, zs - 2, 3, zs - 3, half)]
+    steps = [(dcore, dz) for dz in (1, zs - 1, half, 2, zs - 2, 0, 3, zs - 3) for dcore in range(cs)]
     places, homes = [], []
     for dcore, dz in steps:
         j_core, j_z = wrap(core + dcore, cs), wrap(z + dz, zs)
@@ -53,17 +53,13 @@
         places.append(j_z * cs + j_core)
         homes.append((wrap(j_z + half * across, zs) * cs + j_core, across))
 
+    planes = [wrap(x + dx, xs) * zs * cs for dx in range(xs)]
+
     def each_peer(visit, skip):
         for q in range(len(steps)):
-            if steps[q] not in skip:
-                visit(x * zs * cs, q)
-
-        def plane(dx, carry):
-            for q in range(len(steps)):
-                visit(wrap(x + dx, xs) * zs * cs, q)
-            return carry
-
-        lax.fori_loop(1, xs, plane, 0)
+            for dx in range(xs):
+                if dx or steps[q] not in skip:
+                    visit(planes[dx], q)
 
     t_copy = pltpu.make_async_copy(t_hbm, tv, t_sem)
     t_copy.start()
@@ -76,7 +72,7 @@
         pl.semaphore_signal(barrier, inc=1, device_id=(base + places[q], my), device_id_type=MESH)
 
     each_peer(greet, [(0, 0)])
-    for d in range(1, n_red):
+    for d in (1, 2, n_red - 2, n_red - 1):
         pl.semaphore_signal(barrier, inc=1, device_id=(me, wrap(my + d, n_red)), device_id_type=MESH)
 
     def clear(n, carry):
@@ -108,7 +104,7 @@
         return carry
 
     lax.fori_loop(0, n_j, pack, 0)
-    pl.semaphore_wait(barrier, n_tile + n_red - 2)
+    pl.semaphore_wait(barrier, n_tile - 1 + 4)
 
     own_rows = pl.ds(pl.multiple_of(me * rows, rows), rows)
     own = {}

time: 63 us -> 62.3 us (0.989)
  Pallas kernels: 61 us -> 60.1 us
    pallas_call x1, Pallas kernels: 61 us -> 60.1 us  [local(): pl.pallas_call(functools.partial(kernel, dims, n_tile, n_red), out_shape=...]
where the time goes in v5:
time: 62.3 us; the launch traced here: 61.8 us
  Pallas kernels  60.1 us (96%)
  local copies, waits for them, and re-layouts  1.67 us (3%)
    pallas_call x1, Pallas kernels, local(): pl.pallas_call(functools.partial(kernel, dims, n_tile, n_red), out_shape=...  60.1 us
    unnamed x1, local copies, waits for them, and re-layouts  1.67 us

profile of v5, /device:TPU:1, one launch (start us, length us, event | category | flops | bytes accessed | tf_op | source)
XLA Modules:
  0.0 61.8 jit_solution(12701574135408814593)
XLA Ops:
  0.0 60.1 %shard_map.55 = bf16[128,1024]{1,0:T(8,128)(2,1)} custom-call(s32[2]{0:T(128)} %ck.1, s32[64]{0:T(128)} %cj.1, s32[8]{0:T(128)} %lv.1, bf16[2,64,16,1024]{3,2,1,0:T(8,128)(2,1)} %t_hbm.1, bf16[1024,2,1024]{2,1,0:T(2,128)(2,1)} %w_hbm.1), custom_call_target="tpu_custom_call" | custom-call | flops 2147483648 | bytes 9437184 | tf_op jit(solution)/shard_map/pallas_call | solution.py:283
  60.2 1.7 %copy.7 = bf16[128,1,1024]{2,0,1:T(8,128)(2,1)} copy(bf16[128,1,1024]{2,0,1:T(8,128)(2,1)} %bitcast.1) | data formatting | bytes 524288

commit v6 on v5

--- a/solution.py
+++ b/solution.py
@@ -173,6 +173,7 @@
 
     hops = {}
     first_pair = wrap(my // 2 + n_red // 4, n_red // 2)
+    beside = jnp.where(my - my // 2 * 2 == 1, 1, n_red // 2 - 1)
 
     def multiply(i):
         for copy in own[i]:
@@ -181,7 +182,7 @@
         others = recv[i].at[:, pl.ds(0, n_got * rows), pl.ds(0, TILE)]
         pltpu.make_async_copy(others, others, recv_sem.at[i]).wait()
 
-        def block(n, carry):
+        def block(n):
             pair = wrap(first_pair + n, n_red // 2)
             a_rows = pl.ds(pl.multiple_of(pair * 2 * TILE, 2 * TILE), 2 * TILE)
             acc = jnp.dot(wv[0, a_rows, :], recv[i][0], preferred_element_type=jnp.float32)
@@ -202,13 +203,27 @@
                             device_id=(me, to),
                             device_id_type=MESH,
                         ).start()
+
+        def near(n, carry):
+            block(n * beside)
             return carry
 
-        lax.fori_loop(0, n_red // 2, block, 0)
+        def rest(n, carry):
+            other = n_red // 2 - beside
+            block(other + n * (2 - other))
+            return carry
+
+        lax.fori_loop(0, 2, near, 0)
         if i in TWO_STEP:
-            for slot, to, by in first_step:
-                hops[i, slot] = hop(i, slot, part[i].at[along(to)], by)
-                hops[i, slot].start()
+            depart(i, first_step[:3])
+        lax.fori_loop(0, 2, rest, 0)
+        if i in TWO_STEP:
+            depart(i, first_step[3:])
+
+    def depart(i, which):
+        for slot, to, by in which:
+            hops[i, slot] = hop(i, slot, part[i].at[along(to)], by)
+            hops[i, slot].start()
 
     def combine(i):
         for slot, to, parts in ((5, -2, (0,)), (6, 2, (1, 2))):

time: 62.3 us -> 61 us (0.979)
  Pallas kernels: 60.1 us -> 59.1 us
    pallas_call x1, Pallas kernels: 60.1 us -> 59.1 us  [local(): pl.pallas_call(functools.partial(kernel, dims, n_tile, n_red), out_shape=...]
where the time goes in v6:
time: 61 us; the launch traced here: 60.8 us
  Pallas kernels  59.1 us (97%)
  local copies, waits for them, and re-layouts  1.67 us (3%)
    pallas_call x1, Pallas kernels, local(): pl.pallas_call(functools.partial(kernel, dims, n_tile, n_red), out_shape=...  59.1 us
    unnamed x1, local copies, waits for them, and re-layouts  1.67 us

profile of v6, /device:TPU:1, one launch (start us, length us, event | category | flops | bytes accessed | tf_op | source)
XLA Modules:
  0.0 60.8 jit_solution(13753275206839821964)
XLA Ops:
  0.0 59.1 %shard_map.55 = bf16[128,1024]{1,0:T(8,128)(2,1)} custom-call(s32[2]{0:T(128)} %ck.1, s32[64]{0:T(128)} %cj.1, s32[8]{0:T(128)} %lv.1, bf16[2,64,16,1024]{3,2,1,0:T(8,128)(2,1)} %t_hbm.1, bf16[1024,2,1024]{2,1,0:T(2,128)(2,1)} %w_hbm.1), custom_call_target="tpu_custom_call" | custom-call | flops 2147483648 | bytes 9437184 | tf_op jit(solution)/shard_map/pallas_call | solution.py:298
  59.2 1.7 %copy.7 = bf16[128,1,1024]{2,0,1:T(8,128)(2,1)} copy(bf16[128,1,1024]{2,0,1:T(8,128)(2,1)} %bitcast.1) | data formatting | bytes 524288
